TPU v7x, 32 devices: a whole 2x2x4 slice. The times are simulated.
32 devices in a mesh: lead: 4 (over y, x), dp: 2 (over core), lat: 4 (over z).
Axes of the slice: x: 2, y: 2, z: 4, core: 2. Of those that a mesh axis runs over, the one named last changes fastest.
Arguments:
- field: bfloat16 [4, 16, 32, 64, 128], P('lead', 'dp', 'lat'), may hold values from -6 to 6
- cotangent: bfloat16 [4, 16, 32, 64, 128], P('lead', 'dp', 'lat'), may hold values from -6 to 6
- land_sea: int32 [4, 16, 32, 64], P('lead', 'dp', 'lat'), may hold values from 0 to 1, as said below
- conv1_weight: bfloat16 [3, 3, 128, 128], replicated, may hold values from -0.1875 to 0.1875
- conv1_bias: float32 [128], replicated, may hold values from -3 to 3
- first_norm_scale: float32 [128], replicated, may hold values from 0.5 to 1.5
- norm1_shift: float32 [128], replicated, may hold values from -3 to 3
- conv2_weight: bfloat16 [3, 3, 128, 128], replicated, may hold values from -0.1875 to 0.1875
- conv2_bias: float32 [128], replicated, may hold values from -3 to 3
- second_norm_scale: float32 [128], replicated, may hold values from 0.5 to 1.5
- norm2_shift: float32 [128], replicated, may hold values from -3 to 3
Outputs:
- output: bfloat16 [4, 16, 32, 64, 128], P('lead', 'dp', 'lat')
- field_grad: bfloat16 [4, 16, 32, 64, 128], P('lead', 'dp', 'lat')
- conv1_weight_grad: float32 [3, 3, 128, 128], replicated
- conv1_bias_grad: float32 [128], replicated
- norm1_gain_grad: float32 [128], replicated
- norm1_shift_grad: float32 [128], replicated
- conv2_weight_grad: float32 [3, 3, 128, 128], replicated
- conv2_bias_grad: float32 [128], replicated
- norm2_gain_grad: float32 [128], replicated
- norm2_shift_grad: float32 [128], replicated
Inputs may be any that keep to these rules, and one draw needn't show every extreme that they name: `land_sea`: 1 marks a pixel that counts in the norms, 0 one that is left out.
All inputs are finite; a program needn't handle non-finite values.
Results may differ from a plain program's by a relative error of at most 0.024.
Values may be sent and summed in bfloat16 or wider, within the bound.
No kernel may reach another device: no remote copies, remote signals or barrier semaphores. Data moves between devices by JAX's collectives and lax.ppermute only.
A program may use at most 64 MiB of HBM per device.

v0:
```python
import jax
import jax.numpy as jnp
from jax import lax
from jax.sharding import PartitionSpec as P

EPSILON = 1e-05


def extended(array, sides, width):
    for axis, dim in sides:
        devices, length = (lax.axis_size(axis), array.shape[dim])
        up = [(i, (i + 1) % devices) for i in range(devices - 1)]
        down = [(j, i) for i, j in up]
        last = lax.slice_in_dim(array, length - width, length, axis=dim)
        first = lax.slice_in_dim(array, 0, width, axis=dim)
        before = lax.ppermute(last, axis, up)
        after = lax.ppermute(first, axis, down)
        array = jnp.concatenate([before, array, after], axis=dim)
    return array


def widen(padded):
    return jnp.concatenate([padded[:, :, -1:], padded, padded[:, :, :1]], axis=2)


def convolve(padded, kernel, height, across):
    summed = None
    for tap_row in range(3):
        for tap_col in range(3):
            window = padded[:, tap_row : tap_row + height, tap_col : tap_col + across]
            product = jnp.einsum(
                "srlc,cd->srld",
                window,
                kernel[tap_row, tap_col],
                preferred_element_type=jnp.float32,
            )
            summed = product if summed is None else summed + product
    return summed


def transpose_conv(padded_grad, kernel, height, across):
    summed = None
    for tap_row in range(3):
        for tap_col in range(3):
            window = padded_grad[
                :, 2 - tap_row : 2 - tap_row + height, 2 - tap_col : 2 - tap_col + across
            ]
            product = jnp.einsum(
                "srld,cd->srlc",
                window,
                kernel[tap_row, tap_col],
                preferred_element_type=jnp.float32,
            )
            summed = product if summed is None else summed + product
    return summed


def weight_terms(padded, grad_hidden, height, across):
    partial_terms = []
    for tap_row in range(3):
        for tap_col in range(3):
            window = padded[:, tap_row : tap_row + height, tap_col : tap_col + across]
            partial_terms.append(
                jnp.einsum("srlc,srld->cd", window, grad_hidden, preferred_element_type=jnp.float32)
            )
    channels = grad_hidden.shape[-1]
    return jnp.stack(partial_terms).reshape(3, 3, channels, channels)


def silu_slope(hidden):
    sigmoid_value = jax.nn.sigmoid(hidden)
    return sigmoid_value * (1.0 + hidden * (1.0 - sigmoid_value))


def masked_norm_apply(active, ocean_land_mask, local_count, norm_gain, norm_shift):
    channel_sums, valid_pixel_count = lax.psum(
        (jnp.sum(ocean_land_mask * active, axis=(0, 1, 2)), local_count), ("dp", "lat")
    )
    mean_value = channel_sums / valid_pixel_count
    centred = active - mean_value
    squares = lax.psum(jnp.sum(ocean_land_mask * centred * centred, axis=(0, 1, 2)), ("dp", "lat"))
    variance = squares / valid_pixel_count
    inverse_std = lax.rsqrt(variance + EPSILON)
    normalized = centred * inverse_std
    return (
        ocean_land_mask * (normalized * norm_gain + norm_shift),
        normalized,
        inverse_std,
        valid_pixel_count,
    )


def norm_backward(upstream, ocean_land_mask, normalized, inverse_std, valid_pixel_count, norm_gain):
    masked = ocean_land_mask * upstream
    shift_part = jnp.sum(masked, axis=(0, 1, 2))
    gain_part = jnp.sum(masked * normalized, axis=(0, 1, 2))
    shift_group, gain_group = lax.psum((shift_part, gain_part), ("dp", "lat"))
    correction = norm_gain * (shift_group + normalized * gain_group) / valid_pixel_count
    grad_active = inverse_std * (masked * norm_gain - ocean_land_mask * correction)
    return (grad_active, gain_part, shift_part)


def shards(
    field,
    cotangent,
    land_sea,
    conv1_weight,
    conv1_bias,
    first_norm_scale,
    norm1_shift,
    conv2_weight,
    conv2_bias,
    second_norm_scale,
    norm2_shift,
):
    field_in, cotangent_in, mask_in = (field, cotangent, land_sea)
    inputs = field_in[0]
    upstream = cotangent_in[0]
    ocean_land_mask = mask_in[0].astype(jnp.float32)[..., None]
    height = inputs.shape[1]
    across = inputs.shape[2]
    local_count = jnp.sum(ocean_land_mask)
    padded_in = widen(extended(inputs, (("lat", 1),), 1))
    hidden_one = convolve(padded_in, conv1_weight, height, across) + conv1_bias
    first_normalized, first_standardized, first_inverse_deviation, valid_pixel_count = (
        masked_norm_apply(
            jax.nn.silu(hidden_one), ocean_land_mask, local_count, first_norm_scale, norm1_shift
        )
    )
    padded_mid = widen(extended(first_normalized.astype(jnp.bfloat16), (("lat", 1),), 1))
    hidden_two = convolve(padded_mid, conv2_weight, height, across) + conv2_bias
    second_normalized, second_standardized, second_inverse_deviation, valid_pixel_count = (
        masked_norm_apply(
            jax.nn.silu(hidden_two), ocean_land_mask, local_count, second_norm_scale, norm2_shift
        )
    )
    output = (inputs.astype(jnp.float32) + second_normalized).astype(jnp.bfloat16)
    output_gradient = upstream.astype(jnp.float32)
    grad_active_two, gain_two_part, shift_two_part = norm_backward(
        output_gradient,
        ocean_land_mask,
        second_standardized,
        second_inverse_deviation,
        valid_pixel_count,
        second_norm_scale,
    )
    grad_hidden_two = (grad_active_two * silu_slope(hidden_two)).astype(jnp.bfloat16)
    kernel_two_grad = weight_terms(padded_mid, grad_hidden_two, height, across)
    bias_two_grad = jnp.sum(grad_hidden_two, axis=(0, 1, 2), dtype=jnp.float32)
    first_normalized_gradient = transpose_conv(
        widen(extended(grad_hidden_two, (("lat", 1),), 1)), conv2_weight, height, across
    )
    grad_active_one, gain_one_part, shift_one_part = norm_backward(
        first_normalized_gradient,
        ocean_land_mask,
        first_standardized,
        first_inverse_deviation,
        valid_pixel_count,
        first_norm_scale,
    )
    grad_hidden_one = (grad_active_one * silu_slope(hidden_one)).astype(jnp.bfloat16)
    kernel_one_grad = weight_terms(padded_in, grad_hidden_one, height, across)
    bias_one_grad = jnp.sum(grad_hidden_one, axis=(0, 1, 2), dtype=jnp.float32)
    grad_input = (
        output_gradient
        + transpose_conv(
            widen(extended(grad_hidden_one, (("lat", 1),), 1)), conv1_weight, height, across
        )
    ).astype(jnp.bfloat16)
    all_totals = lax.psum(
        (
            kernel_one_grad,
            bias_one_grad,
            gain_one_part,
            shift_one_part,
            kernel_two_grad,
            bias_two_grad,
            gain_two_part,
            shift_two_part,
        ),
        ("lead", "dp", "lat"),
    )
    output_tile, grad_tile = (output[None], grad_input[None])
    return (
        output_tile,
        grad_tile,
        all_totals[0],
        all_totals[1],
        all_totals[2],
        all_totals[3],
        all_totals[4],
        all_totals[5],
        all_totals[6],
        all_totals[7],
    )


def solution(mesh):
    in_specs = (
        P("lead", "dp", "lat", None, None),
        P("lead", "dp", "lat", None, None),
        P("lead", "dp", "lat", None),
        P(),
        P(),
        P(),
        P(),
        P(),
        P(),
        P(),
        P(),
    )
    out_specs = (
        P("lead", "dp", "lat", None, None),
        P("lead", "dp", "lat", None, None),
        P(),
        P(),
        P(),
        P(),
        P(),
        P(),
        P(),
        P(),
    )
    return jax.shard_map(shards, mesh=mesh, in_specs=in_specs, out_specs=out_specs, check_vma=False)
```

profile of v0, /device:TPU:0, one launch (start us, length us, event | category | flops | bytes accessed | tf_op | source)
XLA Modules:
  0.0 329.7 jit_solution(1622558426462175246)
XLA Ops:
  8.3 4.9 %collective-permute-start = (bf16[8,1,64,128]{3,2,1,0:T(8,128)(2,1)S(1)}, bf16[8,1,64,128]{3,2,1,0:T(8,128)(2,1)S(1)}, u32[]{:S(2)}, u32[]{:S(2)}) collective-permute-start(bf16[8,1,64,128]{3,2,1,0:T(8,128)(2,1)S(1)} %get-tuple-element.63), channel_id=1, source_target_pairs={{0,1},{1,2},{2,3},{4,5},{5,6},{6,7},{8,9},{9,10},{10,11},{12,13},{... | collective-permute-start | bytes 393224 | tf_op jit(solution)/shard_map/ppermute | solution.py:16
  14.6 1.6 fusion.154
  16.8 3.3 collective-permute-done.1
  23.0 3.2 fusion.256
  27.4 1.6 multiply_reduce_fusion.2
  29.0 15.9 %all-reduce.4 = (f32[128]{0:T(128)S(1)}, f32[]{:T(128)}) all-reduce(f32[128]{0:T(128)S(1)} %get-tuple-element.65, f32[]{:T(128)} %convert_reduce_fusion.2), channel_id=1, replica_groups=mesh['lead'=4,'dp'=2,'lat'=4] {'dp','lat'}, use_global_device_ids=true, to_apply=%region_1.2 | all-reduce | flops 129 | bytes 1032 | tf_op jit(solution)/shard_map/psum | solution.py:76
  46.3 14.8 %psum.124 = f32[128]{0:T(128)S(1)} all-reduce(f32[128]{0:T(128)S(1)} %fusion.9), channel_id=1, replica_groups=mesh['lead'=4,'dp'=2,'lat'=4] {'dp','lat'}, use_global_device_ids=true, to_apply=%region_5.6 | all-reduce | flops 128 | bytes 1024 | tf_op jit(solution)/shard_map/psum | solution.py:81
  62.9 3.3 collective-permute-start.2
  67.9 1.5 pad_maximum_fusion.18
  69.4 3.7 %collective-permute-done.3 = bf16[8,1,64,128]{3,2,1,0:T(8,128)(2,1)S(1)} collective-permute-done((bf16[8,1,64,128]{3,2,1,0:T(8,128)(2,1)S(1)}, bf16[8,1,64,128]{3,2,1,0:T(8,128)(2,1)S(1)}, u32[]{:S(2)}, u32[]{:S(2)}) %collective-permute-start.3) | collective-permute-done | bytes 131104 | tf_op jit(solution)/shard_map/ppermute | solution.py:17
  77.1 2.5 multiply_reduce_fusion.1
  79.5 13.7 %psum.125 = f32[128]{0:T(128)S(1)} all-reduce(f32[128]{0:T(128)S(1)} %get-tuple-element.67), channel_id=1, replica_groups=mesh['lead'=4,'dp'=2,'lat'=4] {'dp','lat'}, use_global_device_ids=true, to_apply=%region_7.8 | all-reduce | flops 128 | bytes 1024 | tf_op jit(solution)/shard_map/psum | solution.py:76
  93.9 2.0 fusion.10
  95.9 16.1 %psum.126 = f32[128]{0:T(128)S(1)} all-reduce(f32[128]{0:T(128)S(1)} %fusion.10), channel_id=1, replica_groups=mesh['lead'=4,'dp'=2,'lat'=4] {'dp','lat'}, use_global_device_ids=true, to_apply=%region_9.10 | all-reduce | flops 128 | bytes 1024 | tf_op jit(solution)/shard_map/psum | solution.py:81
  112.7 2.3 fusion.1
  115.0 13.8 %all-reduce.3 = (f32[128]{0:T(128)S(1)}, f32[128]{0:T(128)S(1)}) all-reduce(f32[128]{0:T(128)S(1)} %get-tuple-element.13, f32[128]{0:T(128)S(1)} %get-tuple-element.12), channel_id=1, replica_groups=mesh['lead'=4,'dp'=2,'lat'=4] {'dp','lat'}, use_global_device_ids=true, to_apply=%region_13.14 | all-reduce | flops 256 | bytes 2048 | tf_op jit(solution)/shard_map/psum | solution.py:97
  128.8 4.9 %convert_reduce_fusion = (f32[128]{0:T(128)S(1)}, bf16[8,8,64,128]{3,2,1,0:T(8,128)(2,1)S(1)}, bf16[1,8,8,64,128]{4,3,2,1,0:T(8,128)(2,1)}) fusion(f32[8,8,64,128]{3,2,1,0:T(8,128)} %get-tuple-element.68, f32[]{:T(128)} %get-tuple-element.27, f32[128]{0:T(128)S(1)} %get-tuple-element.24, f32[128]{0:T(128)S(1)} %broadcast_divide_fusion, ...), kind=kLoop, calls=%fused_computation.15 | loop fusion | flops 15728512 | bytes 6311428 | tf_op jit(solution)/shard_map/reduce_sum | solution.py:149
  136.8 1.4 collective-permute-start.5
  138.3 4.7 %collective-permute-start.4 = (bf16[8,1,64,128]{3,2,1,0:T(8,128)(2,1)S(1)}, bf16[8,1,64,128]{3,2,1,0:T(8,128)(2,1)S(1)}, u32[]{:S(2)}, u32[]{:S(2)}) collective-permute-start(bf16[8,1,64,128]{3,2,1,0:T(8,128)(2,1)S(1)} %get-tuple-element.60), channel_id=1, source_target_pairs={{0,1},{1,2},{2,3},{4,5},{5,6},{6,7},{8,9},{9,10},{10,11},{12,13},{... | collective-permute-start | bytes 393224 | tf_op jit(solution)/shard_map/ppermute | solution.py:16
  151.5 2.8 fusion.252
  154.2 15.9 %all-reduce.2 = (f32[128]{0:T(128)S(1)}, f32[128]{0:T(128)S(1)}) all-reduce(f32[128]{0:T(128)S(1)} %get-tuple-element.11, f32[128]{0:T(128)S(1)} %get-tuple-element.10), channel_id=1, replica_groups=mesh['lead'=4,'dp'=2,'lat'=4] {'dp','lat'}, use_global_device_ids=true, to_apply=%region_17.18 | all-reduce | flops 256 | bytes 2048 | tf_op jit(solution)/shard_map/psum | solution.py:97
  170.1 3.5 %convert_reduce_fusion.1 = (f32[128]{0:T(128)S(1)}, bf16[8,8,64,128]{3,2,1,0:T(8,128)(2,1)S(1)}) fusion(f32[8,8,64,128]{3,2,1,0:T(8,128)S(1)} %get-tuple-element.66, f32[]{:T(128)} %get-tuple-element.27, f32[128]{0:T(128)S(1)} %get-tuple-element.22, f32[128]{0:T(128)S(1)} %broadcast_divide_fusion.1, f32[128]{0:T(128)S(1)} %get-tuple-element.23, ...), kind=kLoop, calls=%fused_computation.16 | loop fusion | flops 11534208 | bytes 5262340 | tf_op jit(solution)/shard_map/reduce_sum | solution.py:163
  178.9 1.4 collective-permute-start.7
  180.4 5.2 %collective-permute-start.6 = (bf16[8,1,64,128]{3,2,1,0:T(8,128)(2,1)}, bf16[8,1,64,128]{3,2,1,0:T(8,128)(2,1)}, u32[]{:S(2)}, u32[]{:S(2)}) collective-permute-start(bf16[8,1,64,128]{3,2,1,0:T(8,128)(2,1)} %get-tuple-element.57), channel_id=1, source_target_pairs={{0,1},{1,2},{2,3},{4,5},{5,6},{6,7},{8,9},{9,10},{10,11},{12,13},{... | collective-permute-start | bytes 393224 | tf_op jit(solution)/shard_map/ppermute | solution.py:16
  189.2 38.6 %all-reduce = (f32[128]{0:T(128)}, f32[128]{0:T(128)}, f32[128]{0:T(128)}, f32[128]{0:T(128)}, f32[128]{0:T(128)}, /*index=5*/f32[128]{0:T(128)}) all-reduce(f32[128]{0:T(128)S(1)} %get-tuple-element.30, f32[128]{0:T(128)S(1)} %get-tuple-element.11, ...), channel_id=1, replica_groups=mesh['lead'=4,'dp'=2,'lat'=4] {'lead','dp','lat'}, use_global_device_ids=true, to_apply=%region_20.21 | all-reduce | flops 768 | bytes 6144 | tf_op jit(solution)/shard_map/psum | solution.py:170
  227.8 2.6 fusion.14
  233.4 1.3 fusion.45
  234.8 1.4 fusion.49
  236.2 2.2 fusion.76
  238.4 80.6 %all-reduce.7.cloned.1.call-done = (f32[3,3,128,128]{3,2,1,0:T(8,128)}, f32[3,3,128,128]{3,2,1,0:T(8,128)}) async-done(((f32[3,3,128,128]{3,2,1,0:T(8,128)}, f32[3,3,128,128]{3,2,1,0:T(8,128)}), (f32[3,3,128,128]{3,2,1,0:T(8,128)}, f32[3,3,128,128]{3,2,1,0:T(8,128)})) %all-reduce.7.cloned.1.call-update) | async-done | bytes 1179664 | tf_op jit(solution)/shard_map/psum | solution.py:170
  319.0 1.9 copy.185
  320.9 1.9 copy.186
  (150 shorter events, 40.2 us)
Async XLA Ops:
  7.2 12.9 %copy-start = (bf16[1,8,8,64,128]{4,3,2,1,0:T(8,128)(2,1)S(1)}, bf16[1,8,8,64,128]{4,3,2,1,0:T(8,128)(2,1)}, u32[]{:S(2)}) copy-start(bf16[1,8,8,64,128]{4,3,2,1,0:T(8,128)(2,1)} %param.11) | copy-start | bytes 3145732
  7.2 9.0 %copy-start.31 = (s32[1,8,8,64]{3,2,1,0:T(8,128)S(1)}, s32[1,8,8,64]{3,2,1,0:T(8,128)}, u32[]{:S(2)}) copy-start(s32[1,8,8,64]{3,2,1,0:T(8,128)} %param.13) | copy-start | bytes 49156
  7.2 311.8 %all-reduce.7.cloned.1.call-start = ((), (), s32[]{:S(2)}) async-start(), calls=%async_computation | async-start | bytes 2359296 | tf_op jit(solution)/shard_map/psum | solution.py:170
  8.3 8.5 %collective-permute-start = (bf16[8,1,64,128]{3,2,1,0:T(8,128)(2,1)S(1)}, bf16[8,1,64,128]{3,2,1,0:T(8,128)(2,1)S(1)}, u32[]{:S(2)}, u32[]{:S(2)}) collective-permute-start(bf16[8,1,64,128]{3,2,1,0:T(8,128)(2,1)S(1)} %get-tuple-element.63), channel_id=1, source_target_pairs={{0,1},{1,2},{2,3},{4,5},{5,6},{6,7},{8,9},{9,10},{10,11},{12,13},{... | collective-permute-start | bytes 393224 | tf_op jit(solution)/shard_map/ppermute | solution.py:16
  13.3 6.9 %collective-permute-start.1 = (bf16[8,1,64,128]{3,2,1,0:T(8,128)(2,1)S(1)}, bf16[8,1,64,128]{3,2,1,0:T(8,128)(2,1)S(1)}, u32[]{:S(2)}, u32[]{:S(2)}) collective-permute-start(bf16[8,1,64,128]{3,2,1,0:T(8,128)(2,1)S(1)} %get-tuple-element.64), channel_id=1, source_target_pairs={{1,0},{2,1},{3,2},{5,4},{6,5},{7,6},{9,8},{10,9},{11,10},{13,12},{... | collective-permute-start | bytes 393224 | tf_op jit(solution)/shard_map/ppermute | solution.py:17
  16.8 4.1 %copy-start.11 = (bf16[3,3,128,128]{3,2,1,0:T(8,128)(2,1)S(1)}, bf16[3,3,128,128]{3,2,1,0:T(8,128)(2,1)}, u32[]{:S(2)}) copy-start(bf16[3,3,128,128]{3,2,1,0:T(8,128)(2,1)} %param.14) | copy-start | bytes 884740
  16.8 9.4 %copy-start.17 = (bf16[8,1,64,128]{3,2,1,0:T(8,128)(2,1)}, bf16[8,1,64,128]{3,2,1,0:T(8,128)(2,1)S(1)}, u32[]{:S(2)}) copy-start(bf16[8,1,64,128]{3,2,1,0:T(8,128)(2,1)S(1)} %collective-permute-done) | copy-start | bytes 393220
  20.1 6.6 %copy-start.19 = (bf16[8,1,64,128]{3,2,1,0:T(8,128)(2,1)}, bf16[8,1,64,128]{3,2,1,0:T(8,128)(2,1)S(1)}, u32[]{:S(2)}) copy-start(bf16[8,1,64,128]{3,2,1,0:T(8,128)(2,1)S(1)} %collective-permute-done.1) | copy-start | bytes 393220
  29.0 32.9 %copy-start.32 = (f32[128]{0:T(128)S(1)}, f32[128]{0:T(128)}, u32[]{:S(2)}) copy-start(f32[128]{0:T(128)} %param.16) | copy-start | bytes 1540
  29.0 32.9 %copy-start.35 = (f32[128]{0:T(128)S(1)}, f32[128]{0:T(128)}, u32[]{:S(2)}) copy-start(f32[128]{0:T(128)} %param.17) | copy-start | bytes 1540
  46.3 21.1 %copy-start.10 = (bf16[3,3,128,128]{3,2,1,0:T(8,128)(2,1)S(1)}, bf16[3,3,128,128]{3,2,1,0:T(8,128)(2,1)}, u32[]{:S(2)}) copy-start(bf16[3,3,128,128]{3,2,1,0:T(8,128)(2,1)} %param.18) | copy-start | bytes 884740
  62.8 13.6 %copy-start.1 = (bf16[8,8,64,128]{3,2,1,0:T(8,128)(2,1)}, bf16[8,8,64,128]{3,2,1,0:T(8,128)(2,1)S(1)}, u32[]{:S(2)}) copy-start(bf16[8,8,64,128]{3,2,1,0:T(8,128)(2,1)S(1)} %multiply_convert_fusion.1) | copy-start | bytes 3145732
  62.8 5.1 %copy-start.18 = (bf16[8,1,64,128]{3,2,1,0:T(8,128)(2,1)S(1)}, bf16[8,1,64,128]{3,2,1,0:T(8,128)(2,1)}, u32[]{:S(2)}) copy-start(bf16[8,1,64,128]{3,2,1,0:T(8,128)(2,1)} %copy-done.17) | copy-start | bytes 393220
  62.8 5.1 %copy-start.20 = (bf16[8,1,64,128]{3,2,1,0:T(8,128)(2,1)S(1)}, bf16[8,1,64,128]{3,2,1,0:T(8,128)(2,1)}, u32[]{:S(2)}) copy-start(bf16[8,1,64,128]{3,2,1,0:T(8,128)(2,1)} %copy-done.19) | copy-start | bytes 393220
  62.9 6.5 %collective-permute-start.2 = (bf16[8,1,64,128]{3,2,1,0:T(8,128)(2,1)S(1)}, bf16[8,1,64,128]{3,2,1,0:T(8,128)(2,1)S(1)}, u32[]{:S(2)}, u32[]{:S(2)}) collective-permute-start(bf16[8,1,64,128]{3,2,1,0:T(8,128)(2,1)S(1)} %get-tuple-element.61), channel_id=1, source_target_pairs={{0,1},{1,2},{2,3},{4,5},{5,6},{6,7},{8,9},{9,10},{10,11},{12,13},{... | collective-permute-start | bytes 393224 | tf_op jit(solution)/shard_map/ppermute | solution.py:16
  66.2 6.9 %collective-permute-start.3 = (bf16[8,1,64,128]{3,2,1,0:T(8,128)(2,1)S(1)}, bf16[8,1,64,128]{3,2,1,0:T(8,128)(2,1)S(1)}, u32[]{:S(2)}, u32[]{:S(2)}) collective-permute-start(bf16[8,1,64,128]{3,2,1,0:T(8,128)(2,1)S(1)} %get-tuple-element.62), channel_id=1, source_target_pairs={{1,0},{2,1},{3,2},{5,4},{6,5},{7,6},{9,8},{10,9},{11,10},{13,12},{... | collective-permute-start | bytes 393224 | tf_op jit(solution)/shard_map/ppermute | solution.py:17
  69.4 6.6 %copy-start.13 = (bf16[8,1,64,128]{3,2,1,0:T(8,128)(2,1)}, bf16[8,1,64,128]{3,2,1,0:T(8,128)(2,1)S(1)}, u32[]{:S(2)}) copy-start(bf16[8,1,64,128]{3,2,1,0:T(8,128)(2,1)S(1)} %collective-permute-done.2) | copy-start | bytes 393220
  73.0 3.4 %copy-start.15 = (bf16[8,1,64,128]{3,2,1,0:T(8,128)(2,1)}, bf16[8,1,64,128]{3,2,1,0:T(8,128)(2,1)S(1)}, u32[]{:S(2)}) copy-start(bf16[8,1,64,128]{3,2,1,0:T(8,128)(2,1)S(1)} %collective-permute-done.3) | copy-start | bytes 393220
  73.8 3.0 copy-start.3
  95.9 32.9 %copy-start.36 = (f32[128]{0:T(128)S(1)}, f32[128]{0:T(128)}, u32[]{:S(2)}) copy-start(f32[128]{0:T(128)} %param.20) | copy-start | bytes 1540
  95.9 32.9 %copy-start.37 = (f32[128]{0:T(128)S(1)}, f32[128]{0:T(128)}, u32[]{:S(2)}) copy-start(f32[128]{0:T(128)} %param.21) | copy-start | bytes 1540
  136.8 6.7 %copy-start.2 = (bf16[8,8,64,128]{3,2,1,0:T(8,128)(2,1)S(1)}, bf16[8,8,64,128]{3,2,1,0:T(8,128)(2,1)}, u32[]{:S(2)}) copy-start(bf16[8,8,64,128]{3,2,1,0:T(8,128)(2,1)} %copy-done.1) | copy-start | bytes 3145732
  136.8 6.7 %copy-start.14 = (bf16[8,1,64,128]{3,2,1,0:T(8,128)(2,1)S(1)}, bf16[8,1,64,128]{3,2,1,0:T(8,128)(2,1)}, u32[]{:S(2)}) copy-start(bf16[8,1,64,128]{3,2,1,0:T(8,128)(2,1)} %copy-done.13) | copy-start | bytes 393220
  136.8 6.7 %copy-start.16 = (bf16[8,1,64,128]{3,2,1,0:T(8,128)(2,1)S(1)}, bf16[8,1,64,128]{3,2,1,0:T(8,128)(2,1)}, u32[]{:S(2)}) copy-start(bf16[8,1,64,128]{3,2,1,0:T(8,128)(2,1)} %copy-done.15) | copy-start | bytes 393220
  136.8 10.7 %collective-permute-start.5 = (bf16[8,1,64,128]{3,2,1,0:T(8,128)(2,1)S(1)}, bf16[8,1,64,128]{3,2,1,0:T(8,128)(2,1)S(1)}, u32[]{:S(2)}, u32[]{:S(2)}) collective-permute-start(bf16[8,1,64,128]{3,2,1,0:T(8,128)(2,1)S(1)} %get-tuple-element.59), channel_id=1, source_target_pairs={{1,0},{2,1},{3,2},{5,4},{6,5},{7,6},{9,8},{10,9},{11,10},{13,12},{... | collective-permute-start | bytes 393224 | tf_op jit(solution)/shard_map/ppermute | solution.py:17
  138.3 9.3 %collective-permute-start.4 = (bf16[8,1,64,128]{3,2,1,0:T(8,128)(2,1)S(1)}, bf16[8,1,64,128]{3,2,1,0:T(8,128)(2,1)S(1)}, u32[]{:S(2)}, u32[]{:S(2)}) collective-permute-start(bf16[8,1,64,128]{3,2,1,0:T(8,128)(2,1)S(1)} %get-tuple-element.60), channel_id=1, source_target_pairs={{0,1},{1,2},{2,3},{4,5},{5,6},{6,7},{8,9},{9,10},{10,11},{12,13},{... | collective-permute-start | bytes 393224 | tf_op jit(solution)/shard_map/ppermute | solution.py:16
  170.1 4.3 %copy-start.12 = (bf16[3,3,128,128]{3,2,1,0:T(8,128)(2,1)S(1)}, bf16[3,3,128,128]{3,2,1,0:T(8,128)(2,1)}, u32[]{:S(2)}) copy-start(bf16[3,3,128,128]{3,2,1,0:T(8,128)(2,1)} %param.14) | copy-start | bytes 884740
  173.7 14.1 %copy-start.7 = (bf16[8,8,64,128]{3,2,1,0:T(8,128)(2,1)}, bf16[8,8,64,128]{3,2,1,0:T(8,128)(2,1)S(1)}, u32[]{:S(2)}) copy-start(bf16[8,8,64,128]{3,2,1,0:T(8,128)(2,1)S(1)} %get-tuple-element.31) | copy-start | bytes 3145732
  178.4 7.2 %copy-start.23 = (bf16[8,8,64,128]{3,2,1,0:T(8,128)(2,1)S(1)}, bf16[8,8,64,128]{3,2,1,0:T(8,128)(2,1)}, u32[]{:S(2)}) copy-start(bf16[8,8,64,128]{3,2,1,0:T(8,128)(2,1)} %get-tuple-element.40) | copy-start | bytes 3145732
  178.9 7.1 %copy-start.22 = (bf16[8,8,64,128]{3,2,1,0:T(8,128)(2,1)S(1)}, bf16[8,8,64,128]{3,2,1,0:T(8,128)(2,1)}, u32[]{:S(2)}) copy-start(bf16[8,8,64,128]{3,2,1,0:T(8,128)(2,1)} %get-tuple-element.72) | copy-start | bytes 3145732
  178.9 48.8 %collective-permute-start.7 = (bf16[8,1,64,128]{3,2,1,0:T(8,128)(2,1)}, bf16[8,1,64,128]{3,2,1,0:T(8,128)(2,1)}, u32[]{:S(2)}, u32[]{:S(2)}) collective-permute-start(bf16[8,1,64,128]{3,2,1,0:T(8,128)(2,1)} %get-tuple-element.58), channel_id=1, source_target_pairs={{1,0},{2,1},{3,2},{5,4},{6,5},{7,6},{9,8},{10,9},{11,10},{13,12},{... | collective-permute-start | bytes 393224 | tf_op jit(solution)/shard_map/ppermute | solution.py:17
  180.4 47.4 %collective-permute-start.6 = (bf16[8,1,64,128]{3,2,1,0:T(8,128)(2,1)}, bf16[8,1,64,128]{3,2,1,0:T(8,128)(2,1)}, u32[]{:S(2)}, u32[]{:S(2)}) collective-permute-start(bf16[8,1,64,128]{3,2,1,0:T(8,128)(2,1)} %get-tuple-element.57), channel_id=1, source_target_pairs={{0,1},{1,2},{2,3},{4,5},{5,6},{6,7},{8,9},{9,10},{10,11},{12,13},{... | collective-permute-start | bytes 393224 | tf_op jit(solution)/shard_map/ppermute | solution.py:16
  (15 other events, 18.7 us)
Sparse Core Ops, SparseCore 0:
  189.3 129.6 all-reduce.6
where the time goes:
time: 331 us; the launch traced here: 330 us
  blocking collectives  129 us (39%)
  waiting for transfers between devices  87.6 us (26%)
  matrix products  34.5 us (10%)
  other arithmetic  24.4 us (7%)
  starting transfers between devices  23.6 us (7%)
  local copies, waits for them, and re-layouts  16.1 us (5%)
  between operations  14.8 us (4%)
    psum x1, waiting for transfers between devices, shards(): lax.psum((kernel_one_grad, bias_one_grad, gain_one_part, shift_one_part,...  80.6 us
    psum x1, blocking collectives, shards(): lax.psum((kernel_one_grad, bias_one_grad, gain_one_part, shift_one_part,...  38.6 us
    psum x2, blocking collectives, masked_norm_apply(): lax.psum(jnp.sum(ocean_land_mask * centred * centred, axis=(0, 1, 2)), ('...  30.9 us
    psum x2, blocking collectives, norm_backward(): shift_group, gain_group = lax.psum((shift_part, gain_part), ('dp', 'lat'))  29.7 us
    psum x2, blocking collectives, masked_norm_apply(): lax.psum((jnp.sum(ocean_land_mask * active, axis=(0, 1, 2)), local_count)...  29.6 us
    ppermute x4, starting transfers between devices, extended(): before = lax.ppermute(last, axis, up)  18.1 us
    dot_general x18, matrix products, transpose_conv(): jnp.einsum('srld,cd->srlc', window, kernel[tap_row, tap_col], preferred_e...  13.9 us
    dot_general x18, matrix products, convolve(): jnp.einsum('srlc,cd->srld', window, kernel[tap_row, tap_col], preferred_e...  12 us
  transfers between devices with their start and end apart: 9, of which 3 were waited for; matrix products, arithmetic and copies ran while one was open for 6% of the time, Pallas kernels for 0%

commit v1 on v0

v1 whole, which is shorter than its diff:
```python
import functools

import jax
import jax.numpy as jnp
from jax import lax
from jax.experimental import pallas as pl
from jax.experimental.pallas import tpu as pltpu
from jax.sharding import PartitionSpec as P

EPSILON = 1e-05
BF16 = jnp.bfloat16
F32 = jnp.float32
VMEM = pl.BlockSpec(memory_space=pltpu.VMEM)
SMALL = 16


def fill_toeplitz(taps_ref, out_ref):
    c = taps_ref.shape[-1]
    zero = jnp.zeros((c, c), BF16)
    for b in range(3):
        for i in range(4):
            for j in range(2):
                block = taps_ref[i - j, b] if 0 <= i - j < 3 else zero
                out_ref[b, i * c : (i + 1) * c, j * c : (j + 1) * c] = block


def fill_toeplitz_transposed(taps_ref, out_ref):
    c = taps_ref.shape[-1]
    zero = jnp.zeros((c, c), BF16)
    for b in range(3):
        for i in range(4):
            for j in range(2):
                block = taps_ref[2 - (i - j), 2 - b] if 0 <= i - j < 3 else zero
                out_ref[b, j * c : (j + 1) * c, i * c : (i + 1) * c] = block


def column_sum(products, across):
    shaped = [p.reshape(-1, across, p.shape[-1]) for p in products]
    return (
        pltpu.roll(shaped[0], 1, 1) + shaped[1] + pltpu.roll(shaped[2], across - 1, 1)
    )


def convolve_pairs(row, starts, weights_ref, across, transposed):
    left = jnp.concatenate(
        [jnp.concatenate([row(r - 1 + i) for r in starts], 0) for i in range(4)], 1
    )
    dims = (((1,), (1 if transposed else 0,)), ((), ()))
    return column_sum(
        [
            lax.dot_general(left, weights_ref[b], dims, preferred_element_type=F32)
            for b in range(3)
        ],
        across,
    )


def convolve_single(rows, weights_ref, first, across):
    c = rows[0].shape[-1]
    left = jnp.concatenate(rows, 1)
    low, col = (0, 0) if first else (c, c)
    return column_sum(
        [
            jnp.dot(
                left,
                weights_ref[b, low : low + 3 * c, col : col + c],
                preferred_element_type=F32,
            )
            for b in range(3)
        ],
        across,
    )


def silu_and_slope(hidden):
    gate = 0.5 + 0.5 * jnp.tanh(0.5 * hidden)
    active = hidden * gate
    return active, gate + active * (1.0 - gate)


def silu(value):
    return value * (0.5 + 0.5 * jnp.tanh(0.5 * value))


def fold(value):
    return value.reshape(-1, 8, value.shape[-1]).sum(0)


def norm_terms(stats, count):
    offset = stats[0:1] / count
    variance = jnp.maximum(stats[1:2] / count - offset * offset, 0.0)
    return offset, lax.rsqrt(variance + EPSILON)


def pick(even, when_even, when_odd):
    return jnp.where(even, when_even, when_odd)


def conv1_kernel(x_ref, gx_ref, gp_ref, m_ref, w_ref, b_ref, a_ref, s_ref, st_ref, t_ref):
    samples, height, across, c = x_ref.shape
    even = lax.axis_index("lat") % 2 == 0
    fill_toeplitz(w_ref, t_ref)
    bias = b_ref[...]
    centre = silu(bias)
    sums = [jnp.zeros((8, c), F32) for _ in range(3)]
    for s in range(samples):

        def row(r):
            if r < 0:
                return pick(even, gp_ref[s], gx_ref[s])
            if r >= height:
                return pick(even, gx_ref[s], gp_ref[s])
            return x_ref[s, r]

        out = convolve_pairs(row, range(0, height, 2), t_ref, across, False)
        for j in range(2):
            active, slope = silu_and_slope(out[:, :, j * c : (j + 1) * c] + bias)
            active = active - centre
            for q in range(height // 2):
                r = 2 * q + j
                a_ref[s, r] = active[q]
                s_ref[s, r] = slope[q].astype(BF16)
                mask = m_ref[s, r].astype(F32)
                masked = active[q] * mask
                sums[0] += fold(masked)
                sums[1] += fold(masked * active[q])
                sums[2] += fold(mask)
    total = jnp.concatenate(
        [v.sum(0, keepdims=True) for v in sums] + [jnp.zeros((5, c), F32)], 0
    )
    st_ref[...] = jnp.broadcast_to(total[None], st_ref.shape)


def conv1_edge_kernel(x_ref, gx_ref, gp_ref, hx_ref, hp_ref, w_ref, b_ref, a_ref, s_ref, t_ref):
    samples, height, across, c = x_ref.shape
    even = lax.axis_index("lat") % 2 == 0
    fill_toeplitz(w_ref, t_ref)
    bias = b_ref[...]
    centre = silu(bias)

    def far(ref, s, j):
        at = (s * 3 + j) * across
        return ref[at : at + across]

    def row(r):
        parts = []
        for s in range(samples):
            if r < -1:
                parts.append(pick(even, far(hp_ref, s, r + 4), far(hx_ref, s, r + 4)))
            elif r == -1:
                parts.append(pick(even, gp_ref[s], gx_ref[s]))
            elif r < height:
                parts.append(x_ref[s, r])
            elif r == height:
                parts.append(pick(even, gx_ref[s], gp_ref[s]))
            else:
                j = r - height - 1
                parts.append(pick(even, far(hx_ref, s, j), far(hp_ref, s, j)))
        return jnp.concatenate(parts, 0)

    def put(slot, value):
        active, slope = silu_and_slope(value + bias)
        active = active - centre
        for s in range(samples):
            a_ref[s, slot] = active[s]
            s_ref[s, slot] = slope[s].astype(BF16)

    top = convolve_pairs(row, (-2,), t_ref, across, False)
    put(1, top[:, :, :c])
    put(2, top[:, :, c:])
    bottom = convolve_pairs(row, (height,), t_ref, across, False)
    put(3, bottom[:, :, :c])
    put(4, bottom[:, :, c:])
    put(0, convolve_single([row(r) for r in (-4, -3, -2)], t_ref, False, across))
    put(
        5,
        convolve_single([row(height + r) for r in (1, 2, 3)], t_ref, True, across),
    )


def conv2_kernel(
    st_ref, a_ref, ah_ref, m_ref, mh_ref, u_ref, w_ref, b_ref, g_ref, t_ref,
    n_ref, a2_ref, s2_ref, c1_ref, st2_ref, k_ref,
):
    samples, height, across, c = a_ref.shape
    fill_toeplitz(w_ref, k_ref)
    stats = st_ref[...].sum(0)
    count = stats[2:3]
    offset, inverse = norm_terms(stats, count)
    scale = inverse * g_ref[...]
    shift = t_ref[...] - offset * scale
    c1_ref[...] = jnp.concatenate([offset, inverse, count, jnp.zeros((5, c), F32)], 0)
    bias = b_ref[...]
    centre = silu(bias)
    sums = [jnp.zeros((8, c), F32) for _ in range(4)]
    for s in range(samples):
        for i in range(height + 6):
            r = i - 3
            if r < 0:
                value, mask = ah_ref[s, i], mh_ref[s, i]
            elif r >= height:
                value, mask = ah_ref[s, r - height + 3], mh_ref[s, r - height + 3]
            else:
                value, mask = a_ref[s, r], m_ref[s, r]
            n_ref[s, i] = (value * scale + shift).astype(BF16) * mask

        out = convolve_pairs(
            lambda r: n_ref[s, r + 3], range(-2, height + 2, 2), k_ref, across, False
        )
        for j in range(2):
            active, slope = silu_and_slope(out[:, :, j * c : (j + 1) * c] + bias)
            active = active - centre
            for q in range(height // 2 + 2):
                i = 2 * q + j
                r = i - 2
                a2_ref[s, i] = active[q]
                s2_ref[s, i] = slope[q].astype(BF16)
                if 0 <= r < height:
                    mask = m_ref[s, r].astype(F32)
                    masked = active[q] * mask
                    upstream = u_ref[s, r].astype(F32)
                    sums[0] += fold(masked)
                    sums[1] += fold(masked * active[q])
                    sums[2] += fold(masked * upstream)
                    sums[3] += fold(mask * upstream)
    total = jnp.concatenate(
        [v.sum(0, keepdims=True) for v in sums] + [jnp.zeros((4, c), F32)], 0
    )
    st2_ref[...] = jnp.broadcast_to(total[None], st2_ref.shape)


def back2_kernel(
    st_ref, c1_ref, a2_ref, s2_ref, u_ref, hx_ref, hp_ref, m_ref, mh_ref, a1_ref, w_ref, g_ref, t_ref,
    d_ref, dn_ref, c2_ref, st3_ref, k_ref,
):
    samples, height, across, c = u_ref.shape
    even = lax.axis_index("lat") % 2 == 0
    fill_toeplitz_transposed(w_ref, k_ref)
    stats = st_ref[...].sum(0)
    count = c1_ref[2:3]
    offset, inverse = norm_terms(stats, count)
    shift_sum = stats[3:4]
    gain_sum = inverse * (stats[2:3] - offset * shift_sum)
    scale = inverse * g_ref[...]
    by_active = -scale * gain_sum * inverse / count
    constant = -scale * (shift_sum - offset * inverse * gain_sum) / count
    c2_ref[...] = jnp.concatenate(
        [scale, t_ref[...] - offset * scale, gain_sum, shift_sum, jnp.zeros((4, c), F32)], 0
    )

    def far(ref, s, j):
        at = (samples * 3 + s * 2 + j) * across
        return ref[at : at + across]

    sums = [jnp.zeros((8, c), F32) for _ in range(2)]
    for s in range(samples):
        for i in range(height + 4):
            r = i - 2
            if r < 0:
                upstream, mask = pick(even, far(hp_ref, s, i), far(hx_ref, s, i)), mh_ref[s, i + 1]
            elif r >= height:
                j = r - height
                upstream, mask = pick(even, far(hx_ref, s, j), far(hp_ref, s, j)), mh_ref[s, j + 3]
            else:
                upstream, mask = u_ref[s, r], m_ref[s, r]
            grad = upstream.astype(F32) * scale + (a2_ref[s, i] * by_active + constant)
            d_ref[s, i] = (grad * s2_ref[s, i].astype(F32)).astype(BF16) * mask
        out = convolve_pairs(
            lambda r: d_ref[s, r + 2], range(-1, height + 1, 2), k_ref, across, True
        )
        for j in range(2):
            part = out[:, :, j * c : (j + 1) * c]
            for q in range(height // 2 + 1):
                i = 2 * q + j
                r = i - 1
                dn_ref[s, i] = part[q]
                if 0 <= r < height:
                    masked = part[q] * m_ref[s, r].astype(F32)
                    sums[0] += fold(masked)
                    sums[1] += fold(masked * a1_ref[s, r])
    total = jnp.concatenate(
        [v.sum(0, keepdims=True) for v in sums] + [jnp.zeros((6, c), F32)], 0
    )
    st3_ref[...] = jnp.broadcast_to(total[None], st3_ref.shape)


def weight_products(rows, centre, turned, total_ref, first):
    windows = jnp.concatenate(rows, 1)
    product = lax.dot_general(
        windows,
        jnp.concatenate([turned[0], centre, turned[1]], 1),
        (((0,), (0,)), ((), ())),
        preferred_element_type=F32,
    )
    if first:
        total_ref[...] = product
    else:
        total_ref[...] += product


def turn(value, across):
    c = value.shape[-1]
    return [
        pltpu.roll(value, k, 1).astype(BF16).reshape(-1, c) for k in (across - 1, 1)
    ]


def weight2_kernel(n_ref, d_ref, x_ref, a2_ref, m_ref, c2_ref, o_ref, w_ref, b_ref, acc_ref):
    samples, height, across, c = x_ref.shape
    scale, shift = c2_ref[0:1], c2_ref[1:2]
    bias = jnp.zeros((8, c), F32)
    for s in range(samples):
        grad = d_ref[s, 2 : 2 + height]
        wide = grad.astype(F32)
        bias += fold(wide)
        rows = [n_ref[s, a + 2 : a + 2 + height].reshape(-1, c) for a in range(3)]
        weight_products(rows, grad.reshape(-1, c), turn(wide, across), acc_ref, s == 0)
        for r in range(height):
            normed = (a2_ref[s, r + 2] * scale + shift) * m_ref[s, r].astype(F32)
            o_ref[s, r] = (x_ref[s, r].astype(F32) + normed).astype(BF16)
    b_ref[...] = jnp.broadcast_to(bias.sum(0, keepdims=True), b_ref.shape)
    for a in range(3):
        for b in range(3):
            at = (a * 3 + b) * c
            w_ref[at : at + c] = acc_ref[a * c : (a + 1) * c, b * c : (b + 1) * c].astype(BF16)


def small_rows(rows, c):
    high = jnp.concatenate(rows + [jnp.zeros((8 - len(rows), c), F32)], 0)
    first = high.astype(BF16)
    return jnp.concatenate([first, (high - first.astype(F32)).astype(BF16)], 0)


def weight1_kernel(
    group, leads,
    st_ref, c1_ref, c2_ref, dn_ref, a_ref, ah_ref, s_ref, sh_ref, m_ref, mh_ref,
    x_ref, gx_ref, gp_ref, g_ref, w2_ref, b2_ref,
    d_ref, send_ref, keep_ref, acc_ref,
):
    samples, height, across, c = x_ref.shape
    even = lax.axis_index("lat") % 2 == 0
    lead = lax.axis_index("lead")
    core = lax.axis_index("dp") % 2
    stats = st_ref[...].sum(0)
    offset, inverse, count = c1_ref[0:1], c1_ref[1:2], c1_ref[2:3]
    shift_sum = stats[0:1]
    gain_sum = inverse * (stats[1:2] - offset * shift_sum)
    scale = inverse * g_ref[...]
    by_active = -scale * gain_sum * inverse / count
    constant = -scale * (shift_sum - offset * inverse * gain_sum) / count
    bias = jnp.zeros((8, c), F32)
    for s in range(samples):
        for i in range(height + 2):
            r = i - 1
            if r < 0:
                active, slope, mask = ah_ref[s, 2], sh_ref[s, 2], mh_ref[s, 2]
            elif r >= height:
                active, slope, mask = ah_ref[s, 3], sh_ref[s, 3], mh_ref[s, 3]
            else:
                active, slope, mask = a_ref[s, r], s_ref[s, r], m_ref[s, r]
            grad = dn_ref[s, i] * scale + (active * by_active + constant)
            d_ref[s, i] = (grad * slope.astype(F32)).astype(BF16) * mask
        grad = d_ref[s, 1 : 1 + height]
        wide = grad.astype(F32)
        bias += fold(wide)
        above = pick(even, gp_ref[s], gx_ref[s])
        below = pick(even, gx_ref[s], gp_ref[s])
        body = x_ref[s].reshape(-1, c)
        rows = [
            jnp.concatenate([above, body[: (height - 1) * across]], 0),
            body,
            jnp.concatenate([body[across:], below], 0),
        ]
        weight_products(rows, grad.reshape(-1, c), turn(wide, across), acc_ref, s == 0)

    share = 1.0 / group
    small = [
        small_rows([bias.sum(0, keepdims=True), gain_sum * share, shift_sum * share], c),
        small_rows([b2_ref[0:1], c2_ref[2:3] * share, c2_ref[3:4] * share], c),
    ]

    def put(target, which):
        size = 9 * c // leads
        for j in range(leads):
            slot = j ^ lead
            if which == 1:
                target[slot, :size] = w2_ref[j * size : (j + 1) * size]
            else:
                at = j * size
                while at < (j + 1) * size:
                    tap, low = at // c, at % c
                    step = min(c - low, (j + 1) * size - at)
                    a, b = tap // 3, tap % 3
                    target[slot, at - j * size : at - j * size + step] = acc_ref[
                        a * c + low : a * c + low + step, b * c : (b + 1) * c
                    ].astype(BF16)
                    at += step
            target[slot, size:] = small[which]

    @pl.when(core == 0)
    def _():
        put(keep_ref, 0)
        put(send_ref, 1)

    @pl.when(core != 0)
    def _():
        put(keep_ref, 1)
        put(send_ref, 0)


def input_grad_kernel(d_ref, u_ref, w_ref, o_ref, k_ref):
    samples, height, across, c = u_ref.shape
    fill_toeplitz_transposed(w_ref, k_ref)
    for s in range(samples):
        out = convolve_pairs(
            lambda r: d_ref[s, r + 1], range(0, height, 2), k_ref, across, True
        )
        for q in range(height // 2):
            for j in range(2):
                r = 2 * q + j
                o_ref[s, r] = (
                    u_ref[s, r].astype(F32) + out[q, :, j * c : (j + 1) * c]
                ).astype(BF16)


def call(kernel, outs, scratch, operands, name, flops=0):
    size = sum(o.size * o.dtype.itemsize for o in operands)
    return pl.pallas_call(
        kernel,
        out_shape=outs,
        in_specs=[VMEM] * len(operands),
        out_specs=jax.tree.map(lambda _: VMEM, outs),
        scratch_shapes=scratch,
        compiler_params=pltpu.CompilerParams(vmem_limit_bytes=24 * 2**20),
        cost_estimate=pl.CostEstimate(flops=flops, bytes_accessed=size, transcendentals=0),
        name=name,
    )(*operands)


def swap(value, axis, k):
    return lax.ppermute(value, axis, [(i, i ^ k) for i in range(lax.axis_size(axis))])


def neighbours(value_x, value_p, axis):
    n = lax.axis_size(axis)
    first = [(i, i ^ 1) for i in range(n) if i ^ 1 < n]
    second = [(i, i + 1) for i in range(1, n - 1, 2)]
    second += [(j, i) for i, j in second]
    return lax.ppermute(value_x, axis, first), lax.ppermute(value_p, axis, second)


def spread(stats):
    return lax.all_to_all(stats, ("dp", "lat"), 0, 0)


def add_chunks(parts):
    total = functools.reduce(lambda a, b: a + b, [p.astype(F32) for p in parts])
    size = total.shape[-2] - SMALL
    small = total[..., size : size + 8, :] + total[..., size + 8 :, :]
    high = lax.reduce_precision(small, 8, 7)
    return jnp.concatenate(
        [total[..., :size, :].astype(BF16), high.astype(BF16), (small - high).astype(BF16)], -2
    )


def sum_everywhere(send, keep):
    leads, lats = lax.axis_size("lead"), lax.axis_size("lat")
    chunks = add_chunks([keep, swap(send, "dp", 1)])
    mine = add_chunks([chunks[0]] + [swap(chunks[k], "lead", k) for k in range(1, leads)])
    mine = add_chunks([mine] + [swap(mine, "lat", k) for k in range(1, lats)])
    k = 2
    while k < lax.axis_size("dp"):
        mine = add_chunks([mine, swap(mine, "dp", k)])
        k *= 2
    size = mine.shape[0] - SMALL
    weights = jnp.stack(
        [mine[:size]] + [swap(mine[:size], "lead", k) for k in range(1, leads)]
    ).reshape(-1, mine.shape[-1])
    own = jnp.concatenate([weights, mine[size:]], 0)
    other = swap(own, "dp", 1)
    core = lax.axis_index("dp") % 2
    lead = lax.axis_index("lead")

    def finish(value):
        blocks = value[: leads * size].reshape(leads, size, -1)
        whole = jnp.concatenate(
            [lax.dynamic_index_in_dim(blocks, j ^ lead, 0, False) for j in range(leads)], 0
        )
        c = whole.shape[-1]
        small = value[leads * size :].astype(F32)
        return whole.astype(F32).reshape(3, 3, c, c), small[:8] + small[8:]

    first = finish(jnp.where(core == 0, own, other))
    second = finish(jnp.where(core == 0, other, own))
    return first, second


def shards(
    field,
    cotangent,
    land_sea,
    conv1_weight,
    conv1_bias,
    first_norm_scale,
    norm1_shift,
    conv2_weight,
    conv2_bias,
    second_norm_scale,
    norm2_shift,
):
    x, u, mask = field[0], cotangent[0], land_sea[0]
    samples, height, across, c = x.shape
    pixels = samples * across
    group = lax.axis_size("dp") * lax.axis_size("lat")
    leads = lax.axis_size("lead")
    even = lax.axis_index("lat") % 2 == 0
    vec = lambda v: v.reshape(1, c)
    b1, g1, t1 = vec(conv1_bias), vec(first_norm_scale), vec(norm1_shift)
    b2, g2, t2 = vec(conv2_bias), vec(second_norm_scale), vec(norm2_shift)

    def edge(array, rows, skip, down):
        start = jnp.where(down, height - skip - rows, skip)
        return lax.dynamic_slice_in_dim(array, start, rows, 1)

    bits = mask.astype(BF16)

    def far(down):
        return jnp.concatenate(
            [
                edge(x, 3, 1, down).reshape(-1, c),
                edge(u, 2, 0, down).reshape(-1, c),
                edge(bits, 3, 0, down).reshape(-1, c),
            ],
            0,
        )

    gx, gp = neighbours(
        edge(x, 1, 0, even).reshape(samples, across, c),
        edge(x, 1, 0, ~even).reshape(samples, across, c),
        "lat",
    )
    hx, hp = neighbours(far(even), far(~even), "lat")

    wide_mask = jnp.broadcast_to(bits[..., None], x.shape)

    def halo_bits(far_rows):
        return far_rows[5 * pixels :].reshape(samples, 3, across)

    halo_mask = jnp.concatenate(
        [
            jnp.where(even, halo_bits(hp), halo_bits(hx)),
            jnp.where(even, halo_bits(hx), halo_bits(hp)),
        ],
        1,
    )
    halo_mask = jnp.broadcast_to(halo_mask[..., None], (samples, 6, across, c))

    shape = lambda rows, dtype: jax.ShapeDtypeStruct((samples, rows, across, c), dtype)
    stats_shape = jax.ShapeDtypeStruct((group, 8, c), F32)
    vector = jax.ShapeDtypeStruct((8, c), F32)
    weights = pltpu.VMEM((3, 4 * c, 2 * c), BF16)
    turned = pltpu.VMEM((3, 2 * c, 4 * c), BF16)
    conv_flops = 2 * 9 * c * c * samples * height * across

    a1, s1, st1 = call(
        conv1_kernel,
        (shape(height, F32), shape(height, BF16), stats_shape),
        [weights],
        (x, gx, gp, wide_mask, conv1_weight, b1),
        "conv1",
        conv_flops,
    )
    a1h, s1h = call(
        conv1_edge_kernel,
        (shape(6, F32), shape(6, BF16)),
        [weights],
        (x, gx, gp, hx, hp, conv1_weight, b1),
        "conv1_edges",
        conv_flops,
    )
    st1 = spread(st1)
    n1, a2, s2, c1, st2 = call(
        conv2_kernel,
        (shape(height + 6, BF16), shape(height + 4, F32), shape(height + 4, BF16), vector, stats_shape),
        [weights],
        (st1, a1, a1h, wide_mask, halo_mask, u, conv2_weight, b2, g1, t1),
        "conv2",
        conv_flops,
    )
    st2 = spread(st2)
    d2, dn1, c2, st3 = call(
        back2_kernel,
        (shape(height + 4, BF16), shape(height + 2, F32), vector, stats_shape),
        [turned],
        (st2, c1, a2, s2, u, hx, hp, wide_mask, halo_mask, a1, conv2_weight, g2, t2),
        "conv2_back",
        conv_flops,
    )
    output, w2, bias2 = call(
        weight2_kernel,
        (shape(height, BF16), jax.ShapeDtypeStruct((9 * c, c), BF16), vector),
        [pltpu.VMEM((3 * c, 3 * c), F32)],
        (n1, d2, x, a2, wide_mask, c2),
        "conv2_weight_grad",
        conv_flops,
    )
    st3 = spread(st3)
    chunks = jax.ShapeDtypeStruct((leads, 9 * c // leads + SMALL, c), BF16)
    d1, send, keep = call(
        functools.partial(weight1_kernel, group, leads),
        (shape(height + 2, BF16), chunks, chunks),
        [pltpu.VMEM((3 * c, 3 * c), F32)],
        (st3, c1, c2, dn1, a1, a1h, s1, s1h, wide_mask, halo_mask, x, gx, gp, g1, w2, bias2),
        "conv1_weight_grad",
        conv_flops,
    )
    grad_input = call(
        input_grad_kernel,
        shape(height, BF16),
        [turned],
        (d1, u, conv1_weight),
        "conv1_back",
        conv_flops,
    )
    (k1, small1), (k2, small2) = sum_everywhere(send, keep)
    return (
        output[None],
        grad_input[None],
        k1,
        small1[0],
        small1[1],
        small1[2],
        k2,
        small2[0],
        small2[1],
        small2[2],
    )


def solution(mesh):
    tiles = P("lead", "dp", "lat", None, None)
    in_specs = (tiles, tiles, P("lead", "dp", "lat", None)) + (P(),) * 8
    out_specs = (tiles, tiles) + (P(),) * 8
    return jax.shard_map(shards, mesh=mesh, in_specs=in_specs, out_specs=out_specs, check_vma=False)
```

time: 331 us -> 134 us (0.40)
  blocking collectives: 129 us -> 10.7 us
  waiting for transfers between devices: 87.6 us -> 25.7 us
  matrix products: 34.5 us -> 0 us
  Pallas kernels: 0 us -> 24.1 us
  other arithmetic: 24.4 us -> 5.55 us
  local copies, waits for them, and re-layouts: 16.1 us -> 33.3 us
  between operations: 14.8 us -> 1.19 us
  starting transfers between devices: 23.6 us -> 32.5 us
    psum x7 -> x0, blocking collectives: 129 us -> none  [the longest x1 38.6 us: shards(): lax.psum((kernel_one_grad, bias_one_grad, gain_one_part, shift_one_part,...]
    psum x1 -> x0, waiting for transfers between devices: 80.6 us -> none  [shards(): lax.psum((kernel_one_grad, bias_one_grad, gain_one_part, shift_one_part,...]
    dot_general x54 -> x0, matrix products: 34.5 us -> none  [the longest x18 13.9 us: transpose_conv(): jnp.einsum('srld,cd->srlc', window, kernel[tap_row, tap_col], preferred_e...]
    pallas_call x0 -> x7, Pallas kernels: none -> 24.1 us  [call(): pl.pallas_call(kernel, out_shape=outs, in_specs=[VMEM] * len(operands), o...]
    unnamed x78 -> x86, local copies, waits for them, and re-layouts: 9.79 us -> 29.5 us
    ppermute x8 -> x15, waiting for transfers between devices: 6.95 us -> 25.7 us  [the longest x11 14.7 us: swap(): lax.ppermute(value, axis, [(i, i ^ k) for i in range(lax.axis_size(axis))])]
    reduce_sum x6 -> x0, other arithmetic: 14.2 us -> none  [the longest x1 4.93 us: shards(): bias_two_grad = jnp.sum(grad_hidden_two, axis=(0, 1, 2), dtype=jnp.float32)]
    all_to_all x0 -> x2, starting transfers between devices: none -> 11.5 us  [spread(): return lax.all_to_all(stats, ('dp', 'lat'), 0, 0)]
  transfers between devices with their start and end apart: 9 -> 17, of which waited for: 3 -> 10; matrix products, arithmetic and copies ran while one was open for 6% -> 2% of each run, Pallas kernels for 0% -> 10%
where the time goes in v1:
time: 134 us; the launch traced here: 133 us
  local copies, waits for them, and re-layouts  33.3 us (25%)
  starting transfers between devices  32.5 us (24%)
  waiting for transfers between devices  25.7 us (19%)
  Pallas kernels  24.1 us (18%)
  blocking collectives  10.7 us (8%)
  other arithmetic  5.55 us (4%)
    unnamed x86, local copies, waits for them, and re-layouts  29.5 us
    pallas_call x7, Pallas kernels, call(): pl.pallas_call(kernel, out_shape=outs, in_specs=[VMEM] * len(operands), o...  24.1 us
    ppermute x11, waiting for transfers between devices, swap(): lax.ppermute(value, axis, [(i, i ^ k) for i in range(lax.axis_size(axis))])  14.7 us
    ppermute x11, starting transfers between devices, swap(): lax.ppermute(value, axis, [(i, i ^ k) for i in range(lax.axis_size(axis))])  12.2 us
    all_to_all x2, starting transfers between devices, spread(): return lax.all_to_all(stats, ('dp', 'lat'), 0, 0)  11.5 us
    ppermute x2, waiting for transfers between devices, neighbours(): lax.ppermute(value_x, axis, first)  11 us
    all_to_all x1, blocking collectives, spread(): return lax.all_to_all(stats, ('dp', 'lat'), 0, 0)  10.7 us
    ppermute x2, starting transfers between devices, neighbours(): lax.ppermute(value_x, axis, first)  6.67 us
  transfers between devices with their start and end apart: 17, of which 10 were waited for; matrix products, arithmetic and copies ran while one was open for 2% of the time, Pallas kernels for 10%

profile of v1, /device:TPU:0, one launch (start us, length us, event | category | flops | bytes accessed | tf_op | source)
XLA Modules:
  0.0 133.1 jit_solution(10460514310158750131)
XLA Ops:
  3.7 3.0 %collective-permute-start.2 = (bf16[2572,128]{1,0:T(8,128)(2,1)}, bf16[2572,128]{1,0:T(8,128)(2,1)}, u32[]{:S(2)}, u32[]{:S(2)}) collective-permute-start(bf16[2572,128]{1,0:T(8,128)(2,1)} %pad_maximum_fusion), channel_id=1, source_target_pairs={{0,1},{1,0},{2,3},{3,2},{4,5},{5,4},{6,7},{7,6},{8,9},{9,8},{10,11... | collective-permute-start | bytes 1975304 | tf_op jit(solution)/shard_map/ppermute | solution.py:449
  7.7 1.5 %collective-permute-start.3 = (bf16[2572,128]{1,0:T(8,128)(2,1)}, bf16[2572,128]{1,0:T(8,128)(2,1)}, u32[]{:S(2)}, u32[]{:S(2)}) collective-permute-start(bf16[2572,128]{1,0:T(8,128)(2,1)} %pad_maximum_fusion.1), channel_id=1, source_target_pairs={{1,2},{2,1},{5,6},{6,5},{9,10},{10,9},{13,14},{14,13},{17,18},{18,... | collective-permute-start | bytes 1975304 | tf_op jit(solution)/shard_map/ppermute | solution.py:449
  9.2 3.6 %collective-permute-start = (bf16[8,64,128]{2,1,0:T(8,128)(2,1)S(1)}, bf16[8,64,128]{2,1,0:T(8,128)(2,1)S(1)}, u32[]{:S(2)}, u32[]{:S(2)}) collective-permute-start(bf16[8,64,128]{2,1,0:T(8,128)(2,1)S(1)} %get-tuple-element.57), channel_id=1, source_target_pairs={{0,1},{1,0},{2,3},{3,2},{4,5},{5,4},{6,7},{7,6},{8,9},{9,8},{10,11... | collective-permute-start | bytes 393224 | tf_op jit(solution)/shard_map/ppermute | solution.py:449
  13.6 11.0 %collective-permute-done.gx_ref = bf16[8,64,128]{2,1,0:T(8,128)(2,1)S(1)} collective-permute-done((bf16[8,64,128]{2,1,0:T(8,128)(2,1)S(1)}, bf16[8,64,128]{2,1,0:T(8,128)(2,1)S(1)}, u32[]{:S(2)}, u32[]{:S(2)}) %collective-permute-start) | collective-permute-done | bytes 131104 | tf_op jit(solution)/shard_map/ppermute | solution.py:449
  26.4 3.3 %conv1.1 = (f32[8,8,64,128]{3,2,1,0:T(8,128)S(1)}, bf16[8,8,64,128]{3,2,1,0:T(8,128)(2,1)S(1)}, f32[8,8,128]{2,1,0:T(8,128)}) custom-call(bf16[8,8,64,128]{3,2,1,0:T(8,128)(2,1)S(1)} %bitcast.71, bf16[8,64,128]{2,1,0:T(8,128)(2,1)S(1)} %collective-permute-done.gx_ref, bf16[8,64,128]{2,1,0:T(8,128)(2,1)S(1)} %collective-permute-done.1.gp_ref, ...), custom_call_target="tpu_custom_call" | custom-call | flops 1207959552 | bytes 2654720 | tf_op jit(solution)/shard_map/conv1/pallas_call | solution.py:428
  30.7 8.2 %all-to-all-start = ((f32[8,8,128]{2,1,0:T(8,128)}), f32[8,8,128]{2,1,0:T(8,128)S(1)}, u32[]{:S(2)}, u32[]{:S(2)}) async-start(f32[8,8,128]{2,1,0:T(8,128)} %get-tuple-element.30), calls=%async_computation | async-start | bytes 65536 | tf_op jit(solution)/shard_map/all_to_all | solution.py:453
  43.9 3.3 %conv1_edges.1 = (f32[8,6,64,128]{3,2,1,0:T(8,128)S(1)}, bf16[8,6,64,128]{3,2,1,0:T(8,128)(2,1)S(1)}) custom-call(bf16[8,8,64,128]{3,2,1,0:T(8,128)(2,1)S(1)} %bitcast.72, bf16[8,64,128]{2,1,0:T(8,128)(2,1)S(1)} %copy-done.26, bf16[8,64,128]{2,1,0:T(8,128)(2,1)S(1)} %copy-done.29, bf16[2572,128]{1,0:T(8,128)(2,1)} %collective-permute-done.2.hx_ref, ...), custom_call_target="tpu_custom_call" | custom-call | flops 1207959552 | bytes 2923008 | tf_op jit(solution)/shard_map/conv1_edges/pallas_call | solution.py:428
  49.8 1.5 %copy-done.9 = bf16[1,8,8,64,128]{4,3,2,1,0:T(8,128)(2,1)S(1)} copy-done((bf16[1,8,8,64,128]{4,3,2,1,0:T(8,128)(2,1)S(1)}, bf16[1,8,8,64,128]{4,3,2,1,0:T(8,128)(2,1)}, u32[]{:S(2)}) %copy-start.9) | copy-done | bytes 1048600
  51.3 1.4 %copy-done.12 = f32[8,6,64,128]{3,2,1,0:T(8,128)S(1)} copy-done((f32[8,6,64,128]{3,2,1,0:T(8,128)S(1)}, f32[8,6,64,128]{3,2,1,0:T(8,128)}, u32[]{:S(2)}) %copy-start.12) | copy-done | bytes 1572888
  52.7 4.3 %conv2.1 = (bf16[8,14,64,128]{3,2,1,0:T(8,128)(2,1)S(1)}, f32[8,12,64,128]{3,2,1,0:T(8,128)S(1)}, bf16[8,12,64,128]{3,2,1,0:T(8,128)(2,1)S(1)}, f32[8,128]{1,0:T(8,128)S(1)}, f32[8,8,128]{2,1,0:T(8,128)S(1)}) custom-call(f32[8,8,128]{2,1,0:T(8,128)S(1)} %all-to-all-done.st_ref, f32[8,8,64,128]{3,2,1,0:T(8,128)S(1)} %get-tuple-element.31.a_ref.a1_ref, ...), custom_call_target="tpu_custom_call" | custom-call | flops 1207959552 | bytes 6882816 | tf_op jit(solution)/shard_map/conv2/pallas_call | solution.py:428
  57.1 10.7 %all_to_all.15.st_ref = f32[8,8,128]{2,1,0:T(8,128)S(1)} all-to-all(f32[8,8,128]{2,1,0:T(8,128)S(1)} %get-tuple-element.34), channel_id=1, replica_groups=mesh['lead'=4,'dp'=2,'lat'=4] {'dp','lat'}, dimensions={0} | all-to-all | bytes 65536 | tf_op jit(solution)/shard_map/all_to_all | solution.py:453
  67.8 4.8 %conv2_back.1 = (bf16[8,12,64,128]{3,2,1,0:T(8,128)(2,1)S(1)}, f32[8,10,64,128]{3,2,1,0:T(8,128)S(1)}, f32[8,128]{1,0:T(8,128)S(1)}, f32[8,8,128]{2,1,0:T(8,128)}) custom-call(f32[8,8,128]{2,1,0:T(8,128)S(1)} %all_to_all.15.st_ref, f32[8,128]{1,0:T(8,128)S(1)} %get-tuple-element.35.c1_ref, f32[8,12,64,128]{3,2,1,0:T(8,128)S(1)} %get-tuple-element.36.a2_ref, ...), custom_call_target="tpu_custom_call" | custom-call | flops 1207959552 | bytes 11348992 | tf_op jit(solution)/shard_map/conv2_back/pallas_call | solution.py:428
  72.6 1.5 %copy-done.14 = f32[8,10,64,128]{3,2,1,0:T(8,128)} copy-done((f32[8,10,64,128]{3,2,1,0:T(8,128)}, f32[8,10,64,128]{3,2,1,0:T(8,128)S(1)}, u32[]{:S(2)}) %copy-start.14) | copy-done | bytes 2621464
  75.3 3.3 %all-to-all-start.2 = ((f32[8,8,128]{2,1,0:T(8,128)}), f32[8,8,128]{2,1,0:T(8,128)S(1)}, u32[]{:S(2)}, u32[]{:S(2)}) async-start(f32[8,8,128]{2,1,0:T(8,128)} %get-tuple-element.41), calls=%async_computation.2 | async-start | bytes 65536 | tf_op jit(solution)/shard_map/all_to_all | solution.py:453
  78.6 1.9 %copy-done.3 = f32[8,12,64,128]{3,2,1,0:T(8,128)S(1)} copy-done((f32[8,12,64,128]{3,2,1,0:T(8,128)S(1)}, f32[8,12,64,128]{3,2,1,0:T(8,128)}, u32[]{:S(2)}) %copy-start.3) | copy-done | bytes 3145752
  81.7 1.5 %copy-done.17 = bf16[8,14,64,128]{3,2,1,0:T(8,128)(2,1)S(1)} copy-done((bf16[8,14,64,128]{3,2,1,0:T(8,128)(2,1)S(1)}, bf16[8,14,64,128]{3,2,1,0:T(8,128)(2,1)}, u32[]{:S(2)}) %copy-start.17) | copy-done | bytes 1835032
  83.2 1.4 %copy-done.19 = bf16[8,12,64,128]{3,2,1,0:T(8,128)(2,1)S(1)} copy-done((bf16[8,12,64,128]{3,2,1,0:T(8,128)(2,1)S(1)}, bf16[8,12,64,128]{3,2,1,0:T(8,128)(2,1)}, u32[]{:S(2)}) %copy-start.19) | copy-done | bytes 1572888
  84.7 3.1 %conv2_weight_grad.1 = (bf16[8,8,64,128]{3,2,1,0:T(8,128)(2,1)}, bf16[1152,128]{1,0:T(8,128)(2,1)S(1)}, f32[8,128]{1,0:T(8,128)S(1)}) custom-call(bf16[8,14,64,128]{3,2,1,0:T(8,128)(2,1)S(1)} %copy-done.17, bf16[8,12,64,128]{3,2,1,0:T(8,128)(2,1)S(1)} %copy-done.19, bf16[8,8,64,128]{3,2,1,0:T(8,128)(2,1)S(1)} %bitcast.73, f32[8,12,64,128]{3,2,1,0:T(8,128)S(1)} %copy-done.3, ...), custom_call_target="tpu_custom_call" | custom-call | flops 1207959552 | bytes 8654848 | tf_op jit(solution)/shard_map/conv2_weight_grad/pallas_call | solution.py:428
  90.2 1.4 %copy-done.13 = f32[8,6,64,128]{3,2,1,0:T(8,128)S(1)} copy-done((f32[8,6,64,128]{3,2,1,0:T(8,128)S(1)}, f32[8,6,64,128]{3,2,1,0:T(8,128)}, u32[]{:S(2)}) %copy-start.13) | copy-done | bytes 1572888
  91.6 1.7 %copy-done.15 = f32[8,10,64,128]{3,2,1,0:T(8,128)S(1)} copy-done((f32[8,10,64,128]{3,2,1,0:T(8,128)S(1)}, f32[8,10,64,128]{3,2,1,0:T(8,128)}, u32[]{:S(2)}) %copy-start.15) | copy-done | bytes 2621464
  97.5 2.3 %conv1_weight_grad.1 = (bf16[8,10,64,128]{3,2,1,0:T(8,128)(2,1)S(1)}, bf16[4,304,128]{2,1,0:T(8,128)(2,1)S(1)}, bf16[4,304,128]{2,1,0:T(8,128)(2,1)S(1)}) custom-call(f32[8,8,128]{2,1,0:T(8,128)S(1)} %all-to-all-done.2.st_ref, f32[8,128]{1,0:T(8,128)S(1)} %get-tuple-element.35.c1_ref, f32[8,128]{1,0:T(8,128)S(1)} %get-tuple-element.39.c2_ref, ...), custom_call_target="tpu_custom_call" | custom-call | flops 1207959552 | bytes 11612672 | tf_op jit(solution)/shard_map/conv1_weight_grad/pallas_call | solution.py:428
  101.7 2.5 %collective-permute-start.7 = (bf16[304,128]{1,0:T(8,128)(2,1)S(1)}, bf16[304,128]{1,0:T(8,128)(2,1)S(1)}, u32[]{:S(2)}, u32[]{:S(2)}) collective-permute-start(bf16[304,128]{1,0:T(8,128)(2,1)S(1)} %get-tuple-element.63), channel_id=1, source_target_pairs={{0,24},{8,16},{16,8},{24,0},{1,25},{9,17},{17,9},{25,1},{2,26},{10... | collective-permute-start | bytes 233480 | tf_op jit(solution)/shard_map/ppermute | solution.py:441
  105.3 2.1 %collective-permute-done.7 = bf16[304,128]{1,0:T(8,128)(2,1)S(1)} collective-permute-done((bf16[304,128]{1,0:T(8,128)(2,1)S(1)}, bf16[304,128]{1,0:T(8,128)(2,1)S(1)}, u32[]{:S(2)}, u32[]{:S(2)}) %collective-permute-start.7) | collective-permute-done | bytes 77856 | tf_op jit(solution)/shard_map/ppermute | solution.py:441
  107.3 1.6 %collective-permute-done.6 = bf16[304,128]{1,0:T(8,128)(2,1)S(1)} collective-permute-done((bf16[304,128]{1,0:T(8,128)(2,1)S(1)}, bf16[304,128]{1,0:T(8,128)(2,1)S(1)}, u32[]{:S(2)}, u32[]{:S(2)}) %collective-permute-start.6) | collective-permute-done | bytes 77856 | tf_op jit(solution)/shard_map/ppermute | solution.py:441
  109.2 3.7 %collective-permute-start.10 = (bf16[304,128]{1,0:T(8,128)(2,1)S(1)}, bf16[304,128]{1,0:T(8,128)(2,1)S(1)}, u32[]{:S(2)}, u32[]{:S(2)}) collective-permute-start(bf16[304,128]{1,0:T(8,128)(2,1)S(1)} %pad_maximum_fusion.7), channel_id=1, source_target_pairs={{0,3},{1,2},{2,1},{3,0},{4,7},{5,6},{6,5},{7,4},{8,11},{9,10},{10,... | collective-permute-start | bytes 233480 | tf_op jit(solution)/shard_map/ppermute | solution.py:441
  113.7 2.4 %collective-permute-done.10 = bf16[304,128]{1,0:T(8,128)(2,1)S(1)} collective-permute-done((bf16[304,128]{1,0:T(8,128)(2,1)S(1)}, bf16[304,128]{1,0:T(8,128)(2,1)S(1)}, u32[]{:S(2)}, u32[]{:S(2)}) %collective-permute-start.10) | collective-permute-done | bytes 77856 | tf_op jit(solution)/shard_map/ppermute | solution.py:441
  116.1 3.1 %collective-permute-done.9 = bf16[304,128]{1,0:T(8,128)(2,1)S(1)} collective-permute-done((bf16[304,128]{1,0:T(8,128)(2,1)S(1)}, bf16[304,128]{1,0:T(8,128)(2,1)S(1)}, u32[]{:S(2)}, u32[]{:S(2)}) %collective-permute-start.9) | collective-permute-done | bytes 77856 | tf_op jit(solution)/shard_map/ppermute | solution.py:441
  119.2 1.5 %collective-permute-start.13 = (bf16[288,128]{1,0:T(8,128)(2,1)S(1)}, bf16[288,128]{1,0:T(8,128)(2,1)S(1)}, u32[]{:S(2)}, u32[]{:S(2)}) collective-permute-start(bf16[288,128]{1,0:T(8,128)(2,1)S(1)} %slice.200), channel_id=1, source_target_pairs={{0,24},{8,16},{16,8},{24,0},{1,25},{9,17},{17,9},{25,1},{2,26},{10... | collective-permute-start | bytes 221192 | tf_op jit(solution)/shard_map/ppermute | solution.py:441
  120.8 1.8 %collective-permute-start.12 = (bf16[288,128]{1,0:T(8,128)(2,1)S(1)}, bf16[288,128]{1,0:T(8,128)(2,1)S(1)}, u32[]{:S(2)}, u32[]{:S(2)}) collective-permute-start(bf16[288,128]{1,0:T(8,128)(2,1)S(1)} %slice.200), channel_id=1, source_target_pairs={{0,16},{8,24},{16,0},{24,8},{1,17},{9,25},{17,1},{25,9},{2,18},{10... | collective-permute-start | bytes 221192 | tf_op jit(solution)/shard_map/ppermute | solution.py:441
  122.8 2.4 %collective-permute-done.13 = bf16[288,128]{1,0:T(8,128)(2,1)S(1)} collective-permute-done((bf16[288,128]{1,0:T(8,128)(2,1)S(1)}, bf16[288,128]{1,0:T(8,128)(2,1)S(1)}, u32[]{:S(2)}, u32[]{:S(2)}) %collective-permute-start.13) | collective-permute-done | bytes 73760 | tf_op jit(solution)/shard_map/ppermute | solution.py:441
  125.6 1.4 %collective-permute-done.11 = bf16[288,128]{1,0:T(8,128)(2,1)S(1)} collective-permute-done((bf16[288,128]{1,0:T(8,128)(2,1)S(1)}, bf16[288,128]{1,0:T(8,128)(2,1)S(1)}, u32[]{:S(2)}, u32[]{:S(2)}) %collective-permute-start.11) | collective-permute-done | bytes 73760 | tf_op jit(solution)/shard_map/ppermute | solution.py:441
  127.2 2.9 %conv1_back.1 = bf16[8,8,64,128]{3,2,1,0:T(8,128)(2,1)} custom-call(bf16[8,10,64,128]{3,2,1,0:T(8,128)(2,1)S(1)} %copy-done.37, bf16[8,8,64,128]{3,2,1,0:T(8,128)(2,1)S(1)} %bitcast.77, bf16[3,3,128,128]{3,2,1,0:T(8,128)(2,1)S(1)} %copy-done.40), custom_call_target="tpu_custom_call" | custom-call | flops 1207959552 | bytes 2654208 | tf_op jit(solution)/shard_map/conv1_back/pallas_call | solution.py:428
  (140 shorter events, 31.6 us)
Async XLA Ops:
  2.8 10.8 %copy-start.42 = (s32[1,8,8,64]{3,2,1,0:T(8,128)S(1)}, s32[1,8,8,64]{3,2,1,0:T(8,128)}, u32[]{:S(2)}) copy-start(s32[1,8,8,64]{3,2,1,0:T(8,128)} %param.13) | copy-start | bytes 49156
  3.7 35.2 %collective-permute-start.2 = (bf16[2572,128]{1,0:T(8,128)(2,1)}, bf16[2572,128]{1,0:T(8,128)(2,1)}, u32[]{:S(2)}, u32[]{:S(2)}) collective-permute-start(bf16[2572,128]{1,0:T(8,128)(2,1)} %pad_maximum_fusion), channel_id=1, source_target_pairs={{0,1},{1,0},{2,3},{3,2},{4,5},{5,4},{6,7},{7,6},{8,9},{9,8},{10,11... | collective-permute-start | bytes 1975304 | tf_op jit(solution)/shard_map/ppermute | solution.py:449
  6.8 18.4 %copy-start.38 = (bf16[3,3,128,128]{3,2,1,0:T(8,128)(2,1)S(1)}, bf16[3,3,128,128]{3,2,1,0:T(8,128)(2,1)}, u32[]{:S(2)}) copy-start(bf16[3,3,128,128]{3,2,1,0:T(8,128)(2,1)} %w_ref.9) | copy-start | bytes 884740
  6.8 18.4 %copy-start.41 = (f32[128]{0:T(128)S(1)}, f32[128]{0:T(128)}, u32[]{:S(2)}) copy-start(f32[128]{0:T(128)} %param.15) | copy-start | bytes 1540
  7.7 31.2 %collective-permute-start.3 = (bf16[2572,128]{1,0:T(8,128)(2,1)}, bf16[2572,128]{1,0:T(8,128)(2,1)}, u32[]{:S(2)}, u32[]{:S(2)}) collective-permute-start(bf16[2572,128]{1,0:T(8,128)(2,1)} %pad_maximum_fusion.1), channel_id=1, source_target_pairs={{1,2},{2,1},{5,6},{6,5},{9,10},{10,9},{13,14},{14,13},{17,18},{18,... | collective-permute-start | bytes 1975304 | tf_op jit(solution)/shard_map/ppermute | solution.py:449
  9.2 15.3 %collective-permute-start = (bf16[8,64,128]{2,1,0:T(8,128)(2,1)S(1)}, bf16[8,64,128]{2,1,0:T(8,128)(2,1)S(1)}, u32[]{:S(2)}, u32[]{:S(2)}) collective-permute-start(bf16[8,64,128]{2,1,0:T(8,128)(2,1)S(1)} %get-tuple-element.57), channel_id=1, source_target_pairs={{0,1},{1,0},{2,3},{3,2},{4,5},{5,4},{6,7},{7,6},{8,9},{9,8},{10,11... | collective-permute-start | bytes 393224 | tf_op jit(solution)/shard_map/ppermute | solution.py:449
  12.9 11.7 %collective-permute-start.1 = (bf16[8,64,128]{2,1,0:T(8,128)(2,1)S(1)}, bf16[8,64,128]{2,1,0:T(8,128)(2,1)S(1)}, u32[]{:S(2)}, u32[]{:S(2)}) collective-permute-start(bf16[8,64,128]{2,1,0:T(8,128)(2,1)S(1)} %get-tuple-element.56), channel_id=1, source_target_pairs={{1,2},{2,1},{5,6},{6,5},{9,10},{10,9},{13,14},{14,13},{17,18},{18,... | collective-permute-start | bytes 393224 | tf_op jit(solution)/shard_map/ppermute | solution.py:449
  30.7 18.6 %all-to-all-start = ((f32[8,8,128]{2,1,0:T(8,128)}), f32[8,8,128]{2,1,0:T(8,128)S(1)}, u32[]{:S(2)}, u32[]{:S(2)}) async-start(f32[8,8,128]{2,1,0:T(8,128)} %get-tuple-element.30), calls=%async_computation | async-start | bytes 65536 | tf_op jit(solution)/shard_map/all_to_all | solution.py:453
  43.8 5.9 %copy-start.20 = (bf16[3,3,128,128]{3,2,1,0:T(8,128)(2,1)S(1)}, bf16[3,3,128,128]{3,2,1,0:T(8,128)(2,1)}, u32[]{:S(2)}) copy-start(bf16[3,3,128,128]{3,2,1,0:T(8,128)(2,1)} %w_ref.8) | copy-start | bytes 884740
  43.8 6.0 %copy-start.31 = (f32[128]{0:T(128)S(1)}, f32[128]{0:T(128)}, u32[]{:S(2)}) copy-start(f32[128]{0:T(128)} %param.16) | copy-start | bytes 1540
  43.9 6.0 %copy-start.32 = (f32[128]{0:T(128)S(1)}, f32[128]{0:T(128)}, u32[]{:S(2)}) copy-start(f32[128]{0:T(128)} %param.19) | copy-start | bytes 1540
  43.9 6.0 %copy-start.33 = (f32[128]{0:T(128)S(1)}, f32[128]{0:T(128)}, u32[]{:S(2)}) copy-start(f32[128]{0:T(128)} %param.17) | copy-start | bytes 1540
  49.8 18.0 %copy-start = (bf16[8,6,64,128]{3,2,1,0:T(8,128)(2,1)}, bf16[8,6,64,128]{3,2,1,0:T(8,128)(2,1)S(1)}, u32[]{:S(2)}) copy-start(bf16[8,6,64,128]{3,2,1,0:T(8,128)(2,1)S(1)} %broadcast_in_dim.9.mh_ref) | copy-start | bytes 2359300
  52.7 15.1 %copy-start.34 = (f32[128]{0:T(128)S(1)}, f32[128]{0:T(128)}, u32[]{:S(2)}) copy-start(f32[128]{0:T(128)} %param.20) | copy-start | bytes 1540
  52.7 15.1 %copy-start.35 = (f32[128]{0:T(128)S(1)}, f32[128]{0:T(128)}, u32[]{:S(2)}) copy-start(f32[128]{0:T(128)} %param.21) | copy-start | bytes 1540
  57.1 15.6 %copy-start.2 = (f32[8,12,64,128]{3,2,1,0:T(8,128)}, f32[8,12,64,128]{3,2,1,0:T(8,128)S(1)}, u32[]{:S(2)}) copy-start(f32[8,12,64,128]{3,2,1,0:T(8,128)S(1)} %get-tuple-element.36.a2_ref) | copy-start | bytes 9437188
  57.1 15.5 %copy-start.16 = (bf16[8,14,64,128]{3,2,1,0:T(8,128)(2,1)}, bf16[8,14,64,128]{3,2,1,0:T(8,128)(2,1)S(1)}, u32[]{:S(2)}) copy-start(bf16[8,14,64,128]{3,2,1,0:T(8,128)(2,1)S(1)} %get-tuple-element.33.n_ref) | copy-start | bytes 5505028
  75.3 12.5 %all-to-all-start.2 = ((f32[8,8,128]{2,1,0:T(8,128)}), f32[8,8,128]{2,1,0:T(8,128)S(1)}, u32[]{:S(2)}, u32[]{:S(2)}) async-start(f32[8,8,128]{2,1,0:T(8,128)} %get-tuple-element.41), calls=%async_computation.2 | async-start | bytes 65536 | tf_op jit(solution)/shard_map/all_to_all | solution.py:453
  99.8 1.7 %collective-permute-start.4 = (bf16[4,304,128]{2,1,0:T(8,128)(2,1)S(1)}, bf16[4,304,128]{2,1,0:T(8,128)(2,1)S(1)}, u32[]{:S(2)}, u32[]{:S(2)}) collective-permute-start(bf16[4,304,128]{2,1,0:T(8,128)(2,1)S(1)} %get-tuple-element.49), channel_id=1, source_target_pairs={{0,4},{4,0},{1,5},{5,1},{2,6},{6,2},{3,7},{7,3},{8,12},{12,8},{9,1... | collective-permute-start | bytes 933896 | tf_op jit(solution)/shard_map/ppermute | solution.py:441
  101.7 5.6 %collective-permute-start.7 = (bf16[304,128]{1,0:T(8,128)(2,1)S(1)}, bf16[304,128]{1,0:T(8,128)(2,1)S(1)}, u32[]{:S(2)}, u32[]{:S(2)}) collective-permute-start(bf16[304,128]{1,0:T(8,128)(2,1)S(1)} %get-tuple-element.63), channel_id=1, source_target_pairs={{0,24},{8,16},{16,8},{24,0},{1,25},{9,17},{17,9},{25,1},{2,26},{10... | collective-permute-start | bytes 233480 | tf_op jit(solution)/shard_map/ppermute | solution.py:441
  104.2 4.7 %collective-permute-start.6 = (bf16[304,128]{1,0:T(8,128)(2,1)S(1)}, bf16[304,128]{1,0:T(8,128)(2,1)S(1)}, u32[]{:S(2)}, u32[]{:S(2)}) collective-permute-start(bf16[304,128]{1,0:T(8,128)(2,1)S(1)} %get-tuple-element.64), channel_id=1, source_target_pairs={{0,16},{8,24},{16,0},{24,8},{1,17},{9,25},{17,1},{25,9},{2,18},{10... | collective-permute-start | bytes 233480 | tf_op jit(solution)/shard_map/ppermute | solution.py:441
  104.7 22.4 %copy-start.10 = (bf16[1,8,8,64,128]{4,3,2,1,0:T(8,128)(2,1)S(1)}, bf16[1,8,8,64,128]{4,3,2,1,0:T(8,128)(2,1)}, u32[]{:S(2)}) copy-start(bf16[1,8,8,64,128]{4,3,2,1,0:T(8,128)(2,1)} %param.12) | copy-start | bytes 3145732
  104.7 22.4 %copy-start.37 = (bf16[8,10,64,128]{3,2,1,0:T(8,128)(2,1)S(1)}, bf16[8,10,64,128]{3,2,1,0:T(8,128)(2,1)}, u32[]{:S(2)}) copy-start(bf16[8,10,64,128]{3,2,1,0:T(8,128)(2,1)} %copy-done.36) | copy-start | bytes 3932164
  104.8 22.4 %copy-start.40 = (bf16[3,3,128,128]{3,2,1,0:T(8,128)(2,1)S(1)}, bf16[3,3,128,128]{3,2,1,0:T(8,128)(2,1)}, u32[]{:S(2)}) copy-start(bf16[3,3,128,128]{3,2,1,0:T(8,128)(2,1)} %w_ref.9) | copy-start | bytes 884740
  104.8 4.4 %collective-permute-start.5 = (bf16[304,128]{1,0:T(8,128)(2,1)S(1)}, bf16[304,128]{1,0:T(8,128)(2,1)S(1)}, u32[]{:S(2)}, u32[]{:S(2)}) collective-permute-start(bf16[304,128]{1,0:T(8,128)(2,1)S(1)} %get-tuple-element.62), channel_id=1, source_target_pairs={{0,8},{8,0},{16,24},{24,16},{1,9},{9,1},{17,25},{25,17},{2,10},{10... | collective-permute-start | bytes 233480 | tf_op jit(solution)/shard_map/ppermute | solution.py:441
  109.2 6.8 %collective-permute-start.10 = (bf16[304,128]{1,0:T(8,128)(2,1)S(1)}, bf16[304,128]{1,0:T(8,128)(2,1)S(1)}, u32[]{:S(2)}, u32[]{:S(2)}) collective-permute-start(bf16[304,128]{1,0:T(8,128)(2,1)S(1)} %pad_maximum_fusion.7), channel_id=1, source_target_pairs={{0,3},{1,2},{2,1},{3,0},{4,7},{5,6},{6,5},{7,4},{8,11},{9,10},{10,... | collective-permute-start | bytes 233480 | tf_op jit(solution)/shard_map/ppermute | solution.py:441
  113.0 6.2 %collective-permute-start.9 = (bf16[304,128]{1,0:T(8,128)(2,1)S(1)}, bf16[304,128]{1,0:T(8,128)(2,1)S(1)}, u32[]{:S(2)}, u32[]{:S(2)}) collective-permute-start(bf16[304,128]{1,0:T(8,128)(2,1)S(1)} %pad_maximum_fusion.7), channel_id=1, source_target_pairs={{0,2},{1,3},{2,0},{3,1},{4,6},{5,7},{6,4},{7,5},{8,10},{9,11},{10,... | collective-permute-start | bytes 233480 | tf_op jit(solution)/shard_map/ppermute | solution.py:441
  113.0 6.2 %collective-permute-start.8 = (bf16[304,128]{1,0:T(8,128)(2,1)S(1)}, bf16[304,128]{1,0:T(8,128)(2,1)S(1)}, u32[]{:S(2)}, u32[]{:S(2)}) collective-permute-start(bf16[304,128]{1,0:T(8,128)(2,1)S(1)} %pad_maximum_fusion.7), channel_id=1, source_target_pairs={{0,1},{1,0},{2,3},{3,2},{4,5},{5,4},{6,7},{7,6},{8,9},{9,8},{10,11... | collective-permute-start | bytes 233480 | tf_op jit(solution)/shard_map/ppermute | solution.py:441
  119.2 6.0 %collective-permute-start.13 = (bf16[288,128]{1,0:T(8,128)(2,1)S(1)}, bf16[288,128]{1,0:T(8,128)(2,1)S(1)}, u32[]{:S(2)}, u32[]{:S(2)}) collective-permute-start(bf16[288,128]{1,0:T(8,128)(2,1)S(1)} %slice.200), channel_id=1, source_target_pairs={{0,24},{8,16},{16,8},{24,0},{1,25},{9,17},{17,9},{25,1},{2,26},{10... | collective-permute-start | bytes 221192 | tf_op jit(solution)/shard_map/ppermute | solution.py:441
  120.8 4.8 %collective-permute-start.12 = (bf16[288,128]{1,0:T(8,128)(2,1)S(1)}, bf16[288,128]{1,0:T(8,128)(2,1)S(1)}, u32[]{:S(2)}, u32[]{:S(2)}) collective-permute-start(bf16[288,128]{1,0:T(8,128)(2,1)S(1)} %slice.200), channel_id=1, source_target_pairs={{0,16},{8,24},{16,0},{24,8},{1,17},{9,25},{17,1},{25,9},{2,18},{10... | collective-permute-start | bytes 221192 | tf_op jit(solution)/shard_map/ppermute | solution.py:441
  122.6 4.4 %collective-permute-start.11 = (bf16[288,128]{1,0:T(8,128)(2,1)S(1)}, bf16[288,128]{1,0:T(8,128)(2,1)S(1)}, u32[]{:S(2)}, u32[]{:S(2)}) collective-permute-start(bf16[288,128]{1,0:T(8,128)(2,1)S(1)} %slice.200), channel_id=1, source_target_pairs={{0,8},{8,0},{16,24},{24,16},{1,9},{9,1},{17,25},{25,17},{2,10},{10... | collective-permute-start | bytes 221192 | tf_op jit(solution)/shard_map/ppermute | solution.py:441
  127.0 3.0 %collective-permute-start.14 = (bf16[1168,128]{1,0:T(8,128)(2,1)S(1)}, bf16[1168,128]{1,0:T(8,128)(2,1)S(1)}, u32[]{:S(2)}, u32[]{:S(2)}) collective-permute-start(bf16[1168,128]{1,0:T(8,128)(2,1)S(1)} %pad_maximum_fusion.3), channel_id=1, source_target_pairs={{0,4},{4,0},{1,5},{5,1},{2,6},{6,2},{3,7},{7,3},{8,12},{12,8},{9,1... | collective-permute-start | bytes 897032 | tf_op jit(solution)/shard_map/ppermute | solution.py:441
  (28 other events, 43.9 us)
